TPU v7x, 512 devices: a whole 4x4x16 slice. The times are simulated.
512 devices in a mesh: date: 32 (over y, z_lo), tile: 16 (over x, z_hi, core).
Axes of the slice: x: 4, y: 4, z: 16 (z_hi: 2, z_lo: 8; z = z_hi * 8 + z_lo), core: 2. Of those that a mesh axis runs over, the one named last changes fastest.
Arguments:
- slc: bfloat16 [2, 256, 128, 1024], P(None, 'date', None, 'tile'), may hold values from -40 to 40
Outputs:
- coherence: float32 [2, 256, 512, 256], P(None, 'date', 'tile')
All inputs are finite; a program needn't handle non-finite values.
Results may differ from a plain program's by a relative error of at most 0.0003.
Values may be sent and summed in bfloat16 or wider, within the bound.
No kernel may reach another device: no remote copies, remote signals or barrier semaphores. Data moves between devices by JAX's collectives and lax.ppermute only.
A program may use at most 64 MiB of HBM per device.

v0:
```python
import jax
import jax.numpy as jnp
from jax import lax
from jax.sharding import PartitionSpec as P

LOOK_ROWS = 8
LOOK_COLS = 32


def looked(data):
    lead, count, rows, cols = data.shape
    shaped = data.reshape(lead, count, rows // LOOK_ROWS, LOOK_ROWS, cols // LOOK_COLS, LOOK_COLS)
    shaped = shaped.transpose(0, 1, 2, 4, 3, 5)
    return shaped.reshape(
        lead, count, rows // LOOK_ROWS * (cols // LOOK_COLS), LOOK_ROWS * LOOK_COLS
    )


def look_power(block):
    values = block.astype(jnp.float32)
    return jnp.sum(values * values, axis=(0, 3)) / float(LOOK_ROWS * LOOK_COLS)


def pair_block(mine, mine_power, other, other_power):
    area = float(LOOK_ROWS * LOOK_COLS)
    real_real = jnp.einsum("ack,bck->acb", mine[0], other[0], preferred_element_type=jnp.float32)
    imag_imag = jnp.einsum("ack,bck->acb", mine[1], other[1], preferred_element_type=jnp.float32)
    imag_real = jnp.einsum("ack,bck->acb", mine[1], other[0], preferred_element_type=jnp.float32)
    real_imag = jnp.einsum("ack,bck->acb", mine[0], other[1], preferred_element_type=jnp.float32)
    cross = jnp.stack([real_real + imag_imag, imag_real - real_imag]) / area
    scale = jnp.sqrt(mine_power[:, :, None] * other_power.T[None, :, :] + 1e-06)
    return cross / scale[None]


def on_device(slc):
    tiles = lax.all_to_all(slc, "tile", split_axis=2, concat_axis=3, tiled=True)
    mine = looked(tiles)
    own_power = look_power(mine)
    piece = lax.all_gather(mine, "date", axis=1, tiled=True)
    return pair_block(mine, own_power, piece, look_power(piece))


def solution(mesh):
    in_specs = (P(None, "date", None, "tile"),)
    out_specs = P(None, "date", "tile", None)
    return jax.shard_map(
        on_device, mesh=mesh, in_specs=in_specs, out_specs=out_specs, check_vma=False
    )
```

profile of v0, /device:TPU:2, one launch (start us, length us, event | category | flops | bytes accessed | tf_op | source)
XLA Modules:
  0.0 328.7 jit_solution(7657077471930767839)
XLA Ops:
  6.5 1.4 copy.9
  7.9 0.4 reshape.21
  8.3 32.8 %all_to_all.15 = bf16[16,2,4096]{2,1,0:T(2,128)(2,1)S(1)} all-to-all(bf16[16,2,4096]{2,1,0:T(2,128)(2,1)S(1)} %reshape.21), channel_id=1, replica_groups=mesh['date'=32,'tile'=16] {'tile'}, dimensions={0} | all-to-all | bytes 524288 | tf_op jit(solution)/shard_map/all_to_all | solution.py:36
  41.1 0.3 reshape.22
  41.5 0.3 copy.11
  41.8 0.4 reshape.19
  42.2 0.4 copy.12
  42.6 1.4 reshape.20
  44.1 0.4 multiply_reduce_fusion.1
  44.4 0.1 copy.15
  44.5 0.1 fusion.9
  44.6 0.2 copy.13
  44.8 0.4 squeeze.17
  45.2 0.2 copy.14
  45.4 0.4 squeeze.19
  45.8 264.5 %all-gather.2.cloned.1.call-done = bf16[2,256,32,256]{3,1,2,0:T(8,128)(2,1)} async-done(((bf16[2,8,32,256]{3,1,2,0:T(8,128)(2,1)}), bf16[2,256,32,256]{3,1,2,0:T(8,128)(2,1)}) %all-gather.2.cloned.1.call-update) | async-done | bytes 8388624 | tf_op jit(solution)/shard_map/all_gather | solution.py:39
  310.3 5.3 %multiply_reduce_fusion = f32[256,32]{0,1:T(8,128)S(1)} fusion(bf16[2,256,32,256]{3,1,2,0:T(8,128)(2,1)} %all-gather.2.cloned.1.call-done), kind=kLoop, calls=%fused_computation | loop fusion | flops 12574720 | bytes 8421376 | tf_op jit(solution)/shard_map/reduce_sum | solution.py:21
  315.6 0.1 add_sqrt_fusion
  315.7 0.3 copy-done
  316.1 1.2 fusion.1
  317.2 1.2 fusion
  318.4 1.2 fusion.5
  319.6 1.2 fusion.7
  320.9 1.0 copy.16
  (6 shorter events, 0.1 us)
Async XLA Ops:
  6.5 303.8 %all-gather.2.cloned.1.call-start = ((), (), s32[]{:S(2)}) async-start(), calls=%async_computation.1 | async-start | bytes 8650752 | tf_op jit(solution)/shard_map/all_gather | solution.py:39
  310.3 5.8 %copy-start = (bf16[2,256,32,256]{3,1,2,0:T(8,128)(2,1)S(1)}, bf16[2,256,32,256]{3,1,2,0:T(8,128)(2,1)}, u32[]{:S(2)}) copy-start(bf16[2,256,32,256]{3,1,2,0:T(8,128)(2,1)} %all-gather.2.cloned.1.call-done) | copy-start | bytes 25165828
Sparse Core Ops, SparseCore 0:
  44.2 266.0 all-gather.1
where the time goes:
time: 329 us
  waiting for transfers between devices  265 us (81%)
  blocking collectives  32.8 us (10%)
  between operations  13.5 us (4%)
  local copies, waits for them, and re-layouts  7.25 us (2%)
  other arithmetic  5.85 us (2%)
  matrix products  4.77 us (1%)
    all_gather x1, waiting for transfers between devices, on_device(): piece = lax.all_gather(mine, 'date', axis=1, tiled=True)  265 us
    all_to_all x1, blocking collectives, on_device(): tiles = lax.all_to_all(slc, 'tile', split_axis=2, concat_axis=3, tiled=True)  32.8 us
  transfers between devices with their start and end apart: 1, of which 1 were waited for; matrix products, arithmetic and copies ran while one was open for 1% of the time, Pallas kernels for 0%

commit v1 on v0

v1 whole, which is shorter than its diff:
```python
import jax
import jax.numpy as jnp
from jax import lax
from jax.experimental import pallas as pl
from jax.experimental.pallas import tpu as pltpu
from jax.sharding import PartitionSpec as P

LOOK_ROWS = 8
LOOK_COLS = 32
AREA = float(LOOK_ROWS * LOOK_COLS)
SHIFT = 14.0
DEEPEST = 100.0

VMEM = pl.BlockSpec(memory_space=pltpu.VMEM)


def exchange(x, dates):
    rows = lax.broadcasted_iota(jnp.int32, x.shape, 0)
    lanes = lax.broadcasted_iota(jnp.int32, x.shape, 1)
    height, width = x.shape
    step = dates // 2
    while step:
        low_row = (rows & step) == 0
        low_lane = (lanes & (step * LOOK_COLS)) == 0
        up = pltpu.roll(pltpu.roll(x, height - step, 0), step * LOOK_COLS, 1)
        down = pltpu.roll(pltpu.roll(x, step, 0), width - step * LOOK_COLS, 1)
        x = jnp.where(low_row == low_lane, x, jnp.where(low_row, up, down))
        step //= 2
    return x


def split_looks(x_ref, y_ref):
    parts, dates, cols, rows = x_ref.shape
    for part in range(parts):
        for look in range(cols // LOOK_COLS):
            block = x_ref[part, :, look * LOOK_COLS : (look + 1) * LOOK_COLS, :]
            block = block.reshape(dates * LOOK_COLS, rows).astype(jnp.float32)
            block = exchange(block.T, dates)
            block = block.reshape(rows // LOOK_ROWS, dates, dates * LOOK_COLS)
            y_ref[:, look, part * dates : (part + 1) * dates, :] = block.astype(y_ref.dtype)


def pairs(x_ref, y_ref):
    blocks, both, pixels = x_ref.shape
    dates = both // 2
    count = blocks * dates
    x = x_ref[...].astype(jnp.float32)
    real = x[:, :dates].reshape(count, pixels).astype(jnp.bfloat16)
    imag = x[:, dates:].reshape(count, pixels).astype(jnp.bfloat16)
    one = jnp.concatenate([real, imag], axis=1)
    turned = jnp.concatenate([imag, -real], axis=1)
    dims = (((1,), (1,)), ((), ()))
    cross_real = lax.dot_general(one, one, dims, preferred_element_type=jnp.float32) / AREA
    cross_imag = lax.dot_general(turned, one, dims, preferred_element_type=jnp.float32) / AREA
    i = lax.broadcasted_iota(jnp.int32, (count, count), 0)
    j = lax.broadcasted_iota(jnp.int32, (count, count), 1)
    own = i == j
    diagonal = jnp.where(own, cross_real, 0.0)
    power_i = jnp.sum(diagonal, axis=1, keepdims=True)
    power_j = jnp.sum(diagonal, axis=0, keepdims=True)
    highest = power_i * jnp.max(power_j, axis=1, keepdims=True)
    bound = highest * lax.rsqrt(highest * (highest + 1e-06) + 1e-37)
    depth = jnp.clip(jnp.floor(-0.5 * jnp.log2(bound + 1e-37)), 0.0, DEEPEST)
    scale = lax.rsqrt(power_i * power_j + 1e-06) * jnp.exp2(depth + SHIFT)
    out_real = cross_real * scale
    out_imag = jnp.where(own, depth, cross_imag * scale)
    out = jnp.concatenate(
        [out_real.reshape(blocks, dates, count), out_imag.reshape(blocks, dates, count)], axis=1
    )
    y_ref[...] = out


def spread(x_ref, y_ref):
    looks, both, count = x_ref.shape
    dates = both // 2
    x = x_ref[...]
    first = lax.axis_index("date") * dates
    shape = (looks, dates, count)
    i = lax.broadcasted_iota(jnp.int32, shape, 1)
    j = lax.broadcasted_iota(jnp.int32, shape, 2)
    own = j == i + first
    imag = x[:, dates:]
    depth = jnp.sum(jnp.where(own, imag, 0.0), axis=2, keepdims=True)
    scale = jnp.exp2(-SHIFT - depth)
    y_ref[0] = jnp.swapaxes(x[:, :dates] * scale, 0, 1)
    y_ref[1] = jnp.swapaxes(jnp.where(own, 0.0, imag * scale), 0, 1)


def call(kernel, shape, dtype, x):
    return pl.pallas_call(
        kernel,
        out_shape=jax.ShapeDtypeStruct(shape, dtype),
        in_specs=[VMEM],
        out_specs=VMEM,
        compiler_params=pltpu.CompilerParams(vmem_limit_bytes=32 * 1024 * 1024),
    )(x)


def on_device(slc):
    parts, dates, rows, cols = slc.shape
    blocks = lax.axis_size("date")
    look_rows, looks, pixels = rows // LOOK_ROWS, cols // LOOK_COLS, LOOK_ROWS * LOOK_COLS
    count = blocks * dates
    x = slc.transpose(0, 1, 3, 2)
    x = call(split_looks, (look_rows, looks, parts * dates, pixels), jnp.bfloat16, x)
    x = lax.all_to_all(x, "tile", 0, 0, tiled=True)
    x = x.reshape(blocks, parts * dates, pixels)
    x = lax.all_to_all(x, "date", 0, 0, tiled=True)
    x = call(pairs, (blocks, parts * dates, count), jnp.float32, x)
    x = lax.all_to_all(x.astype(jnp.float16), "date", 0, 0, tiled=True).astype(jnp.float32)
    return call(spread, (parts, dates, blocks, count), jnp.float32, x)


def solution(mesh):
    in_specs = (P(None, "date", None, "tile"),)
    out_specs = P(None, "date", "tile", None)
    return jax.shard_map(
        on_device, mesh=mesh, in_specs=in_specs, out_specs=out_specs, check_vma=False
    )
```

time: 329 us -> 96.7 us (0.29)
  the two profiles are of different devices: /device:TPU:2 before, /device:TPU:1 now
where the time goes in v1:
time: 96.7 us; the launch traced here: 96.5 us
  blocking collectives  92.9 us (96%)
  Pallas kernels  2.58 us (3%)
    all_to_all x1, blocking collectives, on_device(): x = lax.all_to_all(x, 'tile', 0, 0, tiled=True)  35.3 us
    all_to_all x1, blocking collectives, on_device(): x = lax.all_to_all(x, 'date', 0, 0, tiled=True)  33.7 us
    all_to_all x1, blocking collectives, on_device(): lax.all_to_all(x.astype(jnp.float16), 'date', 0, 0, tiled=True)  23.9 us
    pallas_call x3, Pallas kernels, call(): pl.pallas_call(kernel, out_shape=jax.ShapeDtypeStruct(shape, dtype), in_s...  2.58 us

profile of v1, /device:TPU:1, one launch (start us, length us, event | category | flops | bytes accessed | tf_op | source)
XLA Modules:
  0.0 96.5 jit_solution(13350653568073418278)
XLA Ops:
  0.0 0.0 copy-start
  0.0 0.9 copy-done
  1.0 1.0 %shard_map.17 = bf16[16,2,16,256]{3,2,1,0:T(8,128)(2,1)S(1)} custom-call(bf16[2,8,64,128]{3,2,1,0:T(8,128)(2,1)S(1)} %bitcast.2), custom_call_target="tpu_custom_call" | custom-call | tf_op jit(solution)/shard_map/pallas_call | solution.py:90
  2.0 35.3 %all_to_all.15 = bf16[16,2,16,256]{3,2,1,0:T(8,128)(2,1)S(1)} all-to-all(bf16[16,2,16,256]{3,2,1,0:T(8,128)(2,1)S(1)} %shard_map.17), channel_id=1, replica_groups=mesh['date'=32,'tile'=16] {'tile'}, dimensions={0} | all-to-all | bytes 524288 | tf_op jit(solution)/shard_map/all_to_all | solution.py:106
  37.3 33.7 %all_to_all.16.x_ref = bf16[32,16,256]{2,1,0:T(8,128)(2,1)S(1)} all-to-all(bf16[32,16,256]{2,1,0:T(8,128)(2,1)S(1)} %bitcast.3), channel_id=1, replica_groups=mesh['date'=32,'tile'=16] {'date'}, dimensions={0} | all-to-all | bytes 524288 | tf_op jit(solution)/shard_map/all_to_all | solution.py:108
  71.0 0.6 shard_map.18
  71.6 23.9 %all_to_all.17 = f16[32,16,256]{2,1,0:T(8,128)(2,1)S(1)} all-to-all(f16[32,16,256]{2,1,0:T(8,128)(2,1)S(1)} %convert_element_type.6), channel_id=1, replica_groups=mesh['date'=32,'tile'=16] {'date'}, dimensions={0} | all-to-all | bytes 524288 | tf_op jit(solution)/shard_map/all_to_all | solution.py:110
  95.4 0.1 convert_element_type.7.x_ref
  95.5 1.0 %shard_map.19 = f32[2,8,32,256]{3,2,1,0:T(8,128)} custom-call(f32[32,16,256]{2,1,0:T(8,128)S(1)} %convert_element_type.7.x_ref), custom_call_target="tpu_custom_call" | custom-call | tf_op jit(solution)/shard_map/pallas_call | solution.py:90
  (1 shorter events, 0.0 us)
Async XLA Ops:
  0.0 0.9 copy-start

commit v2 on v1

--- a/solution.py
+++ b/solution.py
@@ -10,8 +10,41 @@
 AREA = float(LOOK_ROWS * LOOK_COLS)
 SHIFT = 14.0
 DEEPEST = 100.0
+EXTRA = 16
 
 VMEM = pl.BlockSpec(memory_space=pltpu.VMEM)
+
+
+def place(cross, flip, half):
+    return jnp.where(cross == 1, half * 6 + flip, 2 + half * 2 + flip)
+
+
+def worked_at(look_row, half, tile):
+    y = (look_row // 4 - tile // 4) % 4
+    return y * 8 + place((look_row // 2 % 2) ^ (tile // 2 % 2), (look_row % 2) ^ (tile % 2), half)
+
+
+def found_at(look_col, tile):
+    source, half = look_col // 2, look_col % 2
+    cross = (source // 2 % 2) ^ (tile // 2 % 2)
+    z_lo = place(cross, (source % 2) ^ (tile % 2), half)
+    return (tile // 4 - source // 4) % 4 * 8 + jnp.where(cross == 1, 7 - z_lo, z_lo)
+
+
+def moves():
+    pairs = []
+    for y in range(4):
+        for z_lo in range(8):
+            cross = int(z_lo in (0, 1, 6, 7))
+            flip = z_lo % 2
+            for x in range(4):
+                for z_hi in range(2):
+                    for core in range(2):
+                        here = (y * 8 + z_lo) * 16 + x * 4 + z_hi * 2 + core
+                        date = y * 8 + (7 - z_lo if cross else z_lo)
+                        tile = (x + y) % 4 * 4 + (z_hi ^ cross) * 2 + (core ^ flip)
+                        pairs.append((here, date * 16 + tile))
+    return pairs
 
 
 def exchange(x, dates):
@@ -31,13 +64,18 @@
 
 def split_looks(x_ref, y_ref):
     parts, dates, cols, rows = x_ref.shape
-    for part in range(parts):
-        for look in range(cols // LOOK_COLS):
-            block = x_ref[part, :, look * LOOK_COLS : (look + 1) * LOOK_COLS, :]
+    look_rows = rows // LOOK_ROWS
+    tile = lax.axis_index("tile")
+    for half in range(cols // LOOK_COLS):
+        blocks = []
+        for part in range(parts):
+            block = x_ref[part, :, half * LOOK_COLS : (half + 1) * LOOK_COLS, :]
             block = block.reshape(dates * LOOK_COLS, rows).astype(jnp.float32)
             block = exchange(block.T, dates)
-            block = block.reshape(rows // LOOK_ROWS, dates, dates * LOOK_COLS)
-            y_ref[:, look, part * dates : (part + 1) * dates, :] = block.astype(y_ref.dtype)
+            blocks.append(block.reshape(look_rows, dates, dates * LOOK_COLS))
+        looks = jnp.concatenate(blocks, axis=1).astype(y_ref.dtype)
+        for look_row in range(look_rows):
+            y_ref[worked_at(look_row, half, tile)] = looks[look_row]
 
 
 def pairs(x_ref, y_ref):
@@ -54,26 +92,36 @@
     cross_imag = lax.dot_general(turned, one, dims, preferred_element_type=jnp.float32) / AREA
     i = lax.broadcasted_iota(jnp.int32, (count, count), 0)
     j = lax.broadcasted_iota(jnp.int32, (count, count), 1)
-    own = i == j
-    diagonal = jnp.where(own, cross_real, 0.0)
+    diagonal = jnp.where(i == j, cross_real, 0.0)
     power_i = jnp.sum(diagonal, axis=1, keepdims=True)
     power_j = jnp.sum(diagonal, axis=0, keepdims=True)
-    highest = power_i * jnp.max(power_j, axis=1, keepdims=True)
-    bound = highest * lax.rsqrt(highest * (highest + 1e-06) + 1e-37)
-    depth = jnp.clip(jnp.floor(-0.5 * jnp.log2(bound + 1e-37)), 0.0, DEEPEST)
+    highest = jnp.max(power_j, axis=1, keepdims=True)
+    bound = highest * lax.rsqrt(highest * highest + 1e-06)
+    depth = jnp.clip(jnp.floor(-jnp.log2(bound + 1e-37)), 0.0, DEEPEST)
     scale = lax.rsqrt(power_i * power_j + 1e-06) * jnp.exp2(depth + SHIFT)
-    out_real = cross_real * scale
-    out_imag = jnp.where(own, depth, cross_imag * scale)
-    out = jnp.concatenate(
-        [out_real.reshape(blocks, dates, count), out_imag.reshape(blocks, dates, count)], axis=1
-    )
-    y_ref[...] = out
+    y_ref[:count] = jnp.where(i >= j, cross_real, cross_imag) * scale
+    y_ref[count:] = jnp.broadcast_to(depth, (EXTRA, count))
+
+
+def unfold(x_ref, y_ref):
+    blocks, both, count = y_ref.shape
+    dates = both // 2
+    x = x_ref[:count]
+    depth = x_ref[count : count + 1]
+    turned = x.T
+    i = lax.broadcasted_iota(jnp.int32, (count, count), 0)
+    j = lax.broadcasted_iota(jnp.int32, (count, count), 1)
+    real = jnp.where(i >= j, x, turned)
+    imag = jnp.where(i > j, -turned, jnp.where(i == j, depth, x))
+    y_ref[:, :dates] = real.reshape(blocks, dates, count)
+    y_ref[:, dates:] = imag.reshape(blocks, dates, count)
 
 
 def spread(x_ref, y_ref):
     looks, both, count = x_ref.shape
     dates = both // 2
-    x = x_ref[...]
+    tile = lax.axis_index("tile")
+    x = jnp.stack([x_ref[found_at(look, tile)] for look in range(looks)])
     first = lax.axis_index("date") * dates
     shape = (looks, dates, count)
     i = lax.broadcasted_iota(jnp.int32, shape, 1)
@@ -99,14 +147,14 @@
 def on_device(slc):
     parts, dates, rows, cols = slc.shape
     blocks = lax.axis_size("date")
-    look_rows, looks, pixels = rows // LOOK_ROWS, cols // LOOK_COLS, LOOK_ROWS * LOOK_COLS
+    pixels = LOOK_ROWS * LOOK_COLS
     count = blocks * dates
     x = slc.transpose(0, 1, 3, 2)
-    x = call(split_looks, (look_rows, looks, parts * dates, pixels), jnp.bfloat16, x)
-    x = lax.all_to_all(x, "tile", 0, 0, tiled=True)
-    x = x.reshape(blocks, parts * dates, pixels)
+    x = call(split_looks, (blocks, parts * dates, pixels), jnp.bfloat16, x)
     x = lax.all_to_all(x, "date", 0, 0, tiled=True)
-    x = call(pairs, (blocks, parts * dates, count), jnp.float32, x)
+    x = call(pairs, (count + EXTRA, count), jnp.float32, x)
+    x = lax.ppermute(x.astype(jnp.float16), ("date", "tile"), moves()).astype(jnp.float32)
+    x = call(unfold, (blocks, parts * dates, count), jnp.float32, x)
     x = lax.all_to_all(x.astype(jnp.float16), "date", 0, 0, tiled=True).astype(jnp.float32)
     return call(spread, (parts, dates, blocks, count), jnp.float32, x)
 

time: 96.7 us -> 75.6 us (0.78)
  blocking collectives: 92.9 us -> 60.6 us
  waiting for transfers between devices: 0 us -> 7.79 us
  starting transfers between devices: 0 us -> 3.24 us
    all_to_all x1 -> x0, blocking collectives: 35.3 us -> none  [on_device(): x = lax.all_to_all(x, 'tile', 0, 0, tiled=True)]
    ppermute x0 -> x1, waiting for transfers between devices: none -> 7.79 us  [on_device(): lax.ppermute(x.astype(jnp.float16), ('date', 'tile'), moves())]
    ppermute x0 -> x1, starting transfers between devices: none -> 3.24 us  [on_device(): lax.ppermute(x.astype(jnp.float16), ('date', 'tile'), moves())]
    all_to_all x1, blocking collectives: 23.9 us -> 25.9 us  [on_device(): lax.all_to_all(x.astype(jnp.float16), 'date', 0, 0, tiled=True)]
    pallas_call x3 -> x4, Pallas kernels: 2.58 us -> 2.64 us  [call(): pl.pallas_call(kernel, out_shape=jax.ShapeDtypeStruct(shape, dtype), in_s...]
  transfers between devices with their start and end apart: 0 -> 1, of which waited for: 0 -> 1; matrix products, arithmetic and copies ran while one was open for 0% -> 0% of each run, Pallas kernels for 0% -> 0%
where the time goes in v2:
time: 75.6 us; the launch traced here: 75.4 us
  blocking collectives  60.6 us (80%)
  waiting for transfers between devices  7.79 us (10%)
  starting transfers between devices  3.24 us (4%)
  Pallas kernels  2.64 us (3%)
  local copies, waits for them, and re-layouts  0.95 us (1%)
    all_to_all x1, blocking collectives, on_device(): x = lax.all_to_all(x, 'date', 0, 0, tiled=True)  34.6 us
    all_to_all x1, blocking collectives, on_device(): lax.all_to_all(x.astype(jnp.float16), 'date', 0, 0, tiled=True)  25.9 us
    ppermute x1, waiting for transfers between devices, on_device(): lax.ppermute(x.astype(jnp.float16), ('date', 'tile'), moves())  7.79 us
    ppermute x1, starting transfers between devices, on_device(): lax.ppermute(x.astype(jnp.float16), ('date', 'tile'), moves())  3.24 us
    pallas_call x4, Pallas kernels, call(): pl.pallas_call(kernel, out_shape=jax.ShapeDtypeStruct(shape, dtype), in_s...  2.64 us
  transfers between devices with their start and end apart: 1, of which 1 were waited for; matrix products, arithmetic and copies ran while one was open for 0% of the time, Pallas kernels for 0%

profile of v2, /device:TPU:1, one launch (start us, length us, event | category | flops | bytes accessed | tf_op | source)
XLA Modules:
  0.0 75.4 jit_solution(10679244068526412467)
XLA Ops:
  0.0 0.0 copy-start
  0.0 0.9 %copy-done = bf16[2,8,128,64]{2,3,1,0:T(8,128)(2,1)S(1)} copy-done((bf16[2,8,128,64]{2,3,1,0:T(8,128)(2,1)S(1)}, bf16[2,8,128,64]{2,3,1,0:T(8,128)(2,1)}, u32[]{:S(2)}) %copy-start) | copy-done | bytes 262168
  1.0 1.0 %shard_map.17 = bf16[32,16,256]{2,1,0:T(8,128)(2,1)S(1)} custom-call(bf16[2,8,64,128]{3,2,1,0:T(8,128)(2,1)S(1)} %bitcast.1), custom_call_target="tpu_custom_call" | custom-call | tf_op jit(solution)/shard_map/pallas_call | solution.py:138
  1.9 34.6 %all_to_all.10.x_ref = bf16[32,16,256]{2,1,0:T(8,128)(2,1)S(1)} all-to-all(bf16[32,16,256]{2,1,0:T(8,128)(2,1)S(1)} %shard_map.17), channel_id=1, replica_groups=mesh['date'=32,'tile'=16] {'date'}, dimensions={0} | all-to-all | bytes 524288 | tf_op jit(solution)/shard_map/all_to_all | solution.py:154
  36.6 0.5 shard_map.18
  37.1 3.2 %collective-permute-start = (f16[272,256]{1,0:T(8,128)(2,1)S(1)}, f16[272,256]{1,0:T(8,128)(2,1)S(1)}, u32[]{:S(2)}, u32[]{:S(2)}) collective-permute-start(f16[272,256]{1,0:T(8,128)(2,1)S(1)} %convert_element_type.12), channel_id=1, source_target_pairs={{0,114},{1,115},{2,112},{3,113},{4,118},{5,119},{6,116},{7,117},{8... | collective-permute-start | bytes 417800 | tf_op jit(solution)/shard_map/ppermute | solution.py:156
  40.3 7.8 %collective-permute-done = f16[272,256]{1,0:T(8,128)(2,1)S(1)} collective-permute-done((f16[272,256]{1,0:T(8,128)(2,1)S(1)}, f16[272,256]{1,0:T(8,128)(2,1)S(1)}, u32[]{:S(2)}, u32[]{:S(2)}) %collective-permute-start) | collective-permute-done | bytes 139296 | tf_op jit(solution)/shard_map/ppermute | solution.py:156
  48.1 0.1 shard_map.19
  48.4 25.9 %all_to_all.11 = f16[32,16,256]{2,1,0:T(8,128)(2,1)S(1)} all-to-all(f16[32,16,256]{2,1,0:T(8,128)(2,1)S(1)} %convert_element_type.14), channel_id=1, replica_groups=mesh['date'=32,'tile'=16] {'date'}, dimensions={0} | all-to-all | bytes 524288 | tf_op jit(solution)/shard_map/all_to_all | solution.py:158
  74.3 0.1 convert_element_type.15.x_ref
  74.3 1.0 %shard_map.20 = f32[2,8,32,256]{3,2,1,0:T(8,128)} custom-call(f32[32,16,256]{2,1,0:T(8,128)S(1)} %convert_element_type.15.x_ref), custom_call_target="tpu_custom_call" | custom-call | tf_op jit(solution)/shard_map/pallas_call | solution.py:138
  (3 shorter events, 0.1 us)
Async XLA Ops:
  0.0 0.9 %copy-start = (bf16[2,8,128,64]{2,3,1,0:T(8,128)(2,1)S(1)}, bf16[2,8,128,64]{2,3,1,0:T(8,128)(2,1)}, u32[]{:S(2)}) copy-start(bf16[2,8,128,64]{2,3,1,0:T(8,128)(2,1)} %param.1) | copy-start | bytes 786436
  37.1 11.0 %collective-permute-start = (f16[272,256]{1,0:T(8,128)(2,1)S(1)}, f16[272,256]{1,0:T(8,128)(2,1)S(1)}, u32[]{:S(2)}, u32[]{:S(2)}) collective-permute-start(f16[272,256]{1,0:T(8,128)(2,1)S(1)} %convert_element_type.12), channel_id=1, source_target_pairs={{0,114},{1,115},{2,112},{3,113},{4,118},{5,119},{6,116},{7,117},{8... | collective-permute-start | bytes 417800 | tf_op jit(solution)/shard_map/ppermute | solution.py:156

commit v3 on v1

v3 whole, which is shorter than its diff:
```python
import jax
import jax.numpy as jnp
from jax import lax
from jax.experimental import pallas as pl
from jax.experimental.pallas import tpu as pltpu
from jax.sharding import PartitionSpec as P

LOOK_ROWS = 8
LOOK_COLS = 32
AREA = float(LOOK_ROWS * LOOK_COLS)
SHIFT = 14.0
DEEPEST = 100.0
EXTRA = 8

VMEM = pl.BlockSpec(memory_space=pltpu.VMEM)


def worked_at(look_row, half, tile):
    y = (look_row // 4 - tile // 4) % 4
    cross = (look_row // 2 % 2) ^ (tile // 2 % 2)
    return y * 8 + cross * 4 + half * 2 + ((look_row % 2) ^ (tile % 2))


def found_at(look_col, tile, h):
    source, half = look_col // 2, look_col % 2
    y = (tile // 4 - source // 4) % 4
    p = half * 2 + ((source % 2) ^ (tile % 2))
    cross = (source // 2 % 2) ^ (tile // 2 % 2)
    return y * 4 + p, cross ^ h


def moves(own):
    pairs = []
    for y in range(4):
        for z in range(16):
            h, p = z // 4 % 2, z % 4
            target = (z + (8 * h if own else 4)) % 16
            for x in range(4):
                for core in range(2):
                    here = (y * 8 + z % 8) * 16 + x * 4 + z // 8 * 2 + core
                    there = (y * 8 + target % 8) * 16 + (x + y) % 4 * 4 + target // 8 * 2 + (core ^ (p % 2))
                    pairs.append((here, there))
    return pairs


def quads():
    return [[y * 8 + h * 4 + p for y in range(4) for p in range(4)] for h in range(2)]


def exchange(x, dates):
    rows = lax.broadcasted_iota(jnp.int32, x.shape, 0)
    lanes = lax.broadcasted_iota(jnp.int32, x.shape, 1)
    height, width = x.shape
    step = dates // 2
    while step:
        low_row = (rows & step) == 0
        low_lane = (lanes & (step * LOOK_COLS)) == 0
        up = pltpu.roll(pltpu.roll(x, height - step, 0), step * LOOK_COLS, 1)
        down = pltpu.roll(pltpu.roll(x, step, 0), width - step * LOOK_COLS, 1)
        x = jnp.where(low_row == low_lane, x, jnp.where(low_row, up, down))
        step //= 2
    return x


def split_looks(x_ref, y_ref):
    parts, dates, cols, rows = x_ref.shape
    look_rows = rows // LOOK_ROWS
    tile = lax.axis_index("tile")
    for half in range(cols // LOOK_COLS):
        blocks = []
        for part in range(parts):
            block = x_ref[part, :, half * LOOK_COLS : (half + 1) * LOOK_COLS, :]
            block = block.reshape(dates * LOOK_COLS, rows).astype(jnp.float32)
            block = exchange(block.T, dates)
            blocks.append(block.reshape(look_rows, dates, dates * LOOK_COLS))
        looks = jnp.concatenate(blocks, axis=1).astype(y_ref.dtype)
        for look_row in range(look_rows):
            y_ref[worked_at(look_row, half, tile)] = looks[look_row]


def pairs(x_ref, y_ref):
    blocks, both, pixels = x_ref.shape
    dates = both // 2
    count = blocks * dates // 2
    h = lax.axis_index("date") % 8 // 4
    x = x_ref[...].astype(jnp.float32).reshape(4, 2, 4, both, pixels)
    one, turned, power_i, power_j = [], [], [], []
    dims = (((1,), (1,)), ((), ()))

    def cross(a, b):
        return lax.dot_general(a, b, dims, preferred_element_type=jnp.float32) / AREA

    i = lax.broadcasted_iota(jnp.int32, (count, count), 0)
    j = lax.broadcasted_iota(jnp.int32, (count, count), 1)
    own_real = []
    for q in range(2):
        real = x[:, q, :, :dates].reshape(count, pixels).astype(jnp.bfloat16)
        imag = x[:, q, :, dates:].reshape(count, pixels).astype(jnp.bfloat16)
        one.append(jnp.concatenate([real, imag], axis=1))
        turned.append(jnp.concatenate([imag, -real], axis=1))
        own_real.append(cross(one[q], one[q]))
        diagonal = jnp.where(i == j, own_real[q], 0.0)
        power_i.append(jnp.sum(diagonal, axis=1, keepdims=True))
        power_j.append(jnp.sum(diagonal, axis=0, keepdims=True))
    highest = jnp.max(jnp.maximum(power_j[0], power_j[1]), axis=1, keepdims=True)
    bound = highest * lax.rsqrt(highest * highest + 1e-06)
    depth = jnp.clip(jnp.floor(-jnp.log2(bound + 1e-37)), 0.0, DEEPEST)
    factor = jnp.exp2(depth + SHIFT)
    for q in range(2):
        place = q ^ h
        own = lax.rsqrt(power_i[q] * power_j[q] + 1e-06) * factor
        other = lax.rsqrt(power_i[q] * power_j[1 - q] + 1e-06) * factor
        own_imag = cross(turned[q], one[q])
        y_ref[place, :count] = jnp.where(i >= j, own_real[q], own_imag) * own
        y_ref[place, count : 2 * count] = cross(one[q], one[1 - q]) * other
        y_ref[place, 2 * count : 3 * count] = cross(turned[q], one[1 - q]) * other
        y_ref[place, 3 * count :] = jnp.broadcast_to(depth, (EXTRA, count))


def interleave(own, other, h):
    first = jnp.where(h == 0, own, other)
    second = jnp.where(h == 0, other, own)
    width = own.shape[1]
    step = width // 4
    block = lax.broadcasted_iota(jnp.int32, own.shape, 1) // step

    def by(x, blocks):
        return x if blocks == 0 else pltpu.roll(x, blocks * step % width, 1)

    def choose(a, b, c, d):
        return jnp.where(block < 2, jnp.where(block == 0, a, b), jnp.where(block == 2, c, d))

    low = choose(first, by(second, 1), by(first, 1), by(second, 2))
    high = choose(by(first, 2), by(second, 3), by(first, 3), second)
    return jnp.concatenate([low, high], axis=1)


def unfold(own_ref, other_ref, y_ref):
    peers, rows, _ = y_ref.shape
    dates = rows // 4
    count = peers * dates
    h = lax.axis_index("date") % 8 // 4
    i = lax.broadcasted_iota(jnp.int32, (count, count), 0)
    j = lax.broadcasted_iota(jnp.int32, (count, count), 1)
    for piece, x_ref in enumerate((own_ref, other_ref)):
        x = x_ref[:count]
        depth = x_ref[3 * count : 3 * count + 1]
        flipped = x.T
        real = jnp.where(i >= j, x, flipped)
        imag = jnp.where(i > j, -flipped, jnp.where(i == j, depth, x))
        real = interleave(real, x_ref[count : 2 * count], h)
        imag = interleave(imag, x_ref[2 * count : 3 * count], h)
        first = piece * 2 * dates
        y_ref[:, first : first + dates] = real.reshape(peers, dates, 2 * count)
        y_ref[:, first + dates : first + 2 * dates] = imag.reshape(peers, dates, 2 * count)


def spread(x_ref, y_ref):
    looks, both, count = x_ref.shape
    dates = both // 2
    tile, date = lax.axis_index("tile"), lax.axis_index("date")
    h = date % 8 // 4
    rows = []
    for look in range(looks):
        source, piece = found_at(look, tile, h)
        rows.append(x_ref[source * 2 + piece])
    x = jnp.stack(rows)
    shape = (looks, dates, count)
    i = lax.broadcasted_iota(jnp.int32, shape, 1)
    j = lax.broadcasted_iota(jnp.int32, shape, 2)
    own = j == i + date * dates
    imag = x[:, dates:]
    depth = jnp.sum(jnp.where(own, imag, 0.0), axis=2, keepdims=True)
    scale = jnp.exp2(-SHIFT - depth)
    y_ref[0] = jnp.swapaxes(x[:, :dates] * scale, 0, 1)
    y_ref[1] = jnp.swapaxes(jnp.where(own, 0.0, imag * scale), 0, 1)


def call(kernel, shape, dtype, *xs):
    return pl.pallas_call(
        kernel,
        out_shape=jax.ShapeDtypeStruct(shape, dtype),
        in_specs=[VMEM] * len(xs),
        out_specs=VMEM,
        compiler_params=pltpu.CompilerParams(vmem_limit_bytes=32 * 1024 * 1024),
    )(*xs)


def on_device(slc):
    parts, dates, rows, cols = slc.shape
    blocks = lax.axis_size("date")
    pixels = LOOK_ROWS * LOOK_COLS
    count = blocks * dates
    x = slc.transpose(0, 1, 3, 2)
    x = call(split_looks, (blocks, parts * dates, pixels), jnp.bfloat16, x)
    x = lax.all_to_all(x, "date", 0, 0, tiled=True)
    x = call(pairs, (2, 3 * count // 2 + EXTRA, count // 2), jnp.float32, x)
    other = lax.ppermute(x[1].astype(jnp.float16), ("date", "tile"), moves(False))
    own = lax.ppermute(x[0].astype(jnp.float16), ("date", "tile"), moves(True))
    x = call(
        unfold,
        (blocks // 2, 2 * parts * dates, count),
        jnp.float32,
        own.astype(jnp.float32),
        other.astype(jnp.float32),
    )
    x = lax.all_to_all(x.astype(jnp.float16), "date", 0, 0, axis_index_groups=quads(), tiled=True)
    x = x.astype(jnp.float32).reshape(blocks, parts * dates, count)
    return call(spread, (parts, dates, blocks, count), jnp.float32, x)


def solution(mesh):
    in_specs = (P(None, "date", None, "tile"),)
    out_specs = P(None, "date", "tile", None)
    return jax.shard_map(
        on_device, mesh=mesh, in_specs=in_specs, out_specs=out_specs, check_vma=False
    )
```

time: 96.7 us -> 74.1 us (0.77)
  the two profiles are of different devices: /device:TPU:1 before, /device:TPU:128 now
where the time goes in v3:
time: 74.1 us; the launch traced here: 73.9 us
  blocking collectives  45.8 us (62%)
  starting transfers between devices  14.9 us (20%)
  waiting for transfers between devices  8.88 us (12%)
  Pallas kernels  3.07 us (4%)
  local copies, waits for them, and re-layouts  0.99 us (1%)
    all_to_all x1, blocking collectives, on_device(): x = lax.all_to_all(x, 'date', 0, 0, tiled=True)  27.9 us
    all_to_all x1, blocking collectives, on_device(): lax.all_to_all(x.astype(jnp.float16), 'date', 0, 0, axis_index_groups=qua...  17.9 us
    ppermute x1, waiting for transfers between devices, on_device(): own = lax.ppermute(x[0].astype(jnp.float16), ('date', 'tile'), moves(True))  8.85 us
    ppermute x1, starting transfers between devices, on_device(): lax.ppermute(x[1].astype(jnp.float16), ('date', 'tile'), moves(False))  8.58 us
    ppermute x1, starting transfers between devices, on_device(): own = lax.ppermute(x[0].astype(jnp.float16), ('date', 'tile'), moves(True))  6.35 us
    pallas_call x4, Pallas kernels, call(): pl.pallas_call(kernel, out_shape=jax.ShapeDtypeStruct(shape, dtype), in_s...  3.07 us
  transfers between devices with their start and end apart: 2, of which 1 were waited for; matrix products, arithmetic and copies ran while one was open for 0% of the time, Pallas kernels for 0%

profile of v3, /device:TPU:128, one launch (start us, length us, event | category | flops | bytes accessed | tf_op | source)
XLA Modules:
  0.0 73.9 jit_solution(12557292777891465091)
XLA Ops:
  0.0 0.0 copy-start
  0.0 0.9 %copy-done = bf16[2,8,128,64]{2,3,1,0:T(8,128)(2,1)S(1)} copy-done((bf16[2,8,128,64]{2,3,1,0:T(8,128)(2,1)S(1)}, bf16[2,8,128,64]{2,3,1,0:T(8,128)(2,1)}, u32[]{:S(2)}) %copy-start) | copy-done | bytes 262168
  1.0 1.0 %shard_map.17 = bf16[32,16,256]{2,1,0:T(8,128)(2,1)S(1)} custom-call(bf16[2,8,64,128]{3,2,1,0:T(8,128)(2,1)S(1)} %bitcast.7), custom_call_target="tpu_custom_call" | custom-call | tf_op jit(solution)/shard_map/pallas_call | solution.py:180
  1.9 27.9 %all_to_all.10.x_ref = bf16[32,16,256]{2,1,0:T(8,128)(2,1)S(1)} all-to-all(bf16[32,16,256]{2,1,0:T(8,128)(2,1)S(1)} %shard_map.17), channel_id=1, replica_groups=mesh['date'=32,'tile'=16] {'date'}, dimensions={0} | all-to-all | bytes 524288 | tf_op jit(solution)/shard_map/all_to_all | solution.py:196
  29.8 0.4 shard_map.18
  30.4 8.6 %collective-permute-start.1 = (f16[392,128]{1,0:T(8,128)(2,1)S(1)}, f16[392,128]{1,0:T(8,128)(2,1)S(1)}, u32[]{:S(2)}, u32[]{:S(2)}) collective-permute-start(f16[392,128]{1,0:T(8,128)(2,1)S(1)} %get-tuple-element.5), channel_id=1, source_target_pairs={{0,64},{1,65},{4,68},{5,69},{8,72},{9,73},{12,76},{13,77},{16,81},... | collective-permute-start | bytes 301064 | tf_op jit(solution)/shard_map/ppermute | solution.py:198
  39.0 6.4 %collective-permute-start = (f16[392,128]{1,0:T(8,128)(2,1)S(1)}, f16[392,128]{1,0:T(8,128)(2,1)S(1)}, u32[]{:S(2)}, u32[]{:S(2)}) collective-permute-start(f16[392,128]{1,0:T(8,128)(2,1)S(1)} %get-tuple-element.6), channel_id=1, source_target_pairs={{0,0},{1,1},{4,4},{5,5},{8,8},{9,9},{12,12},{13,13},{16,17},{17,16... | collective-permute-start | bytes 301064 | tf_op jit(solution)/shard_map/ppermute | solution.py:199
  45.3 0.0 collective-permute-done.1
  45.4 8.8 %collective-permute-done = f16[392,128]{1,0:T(8,128)(2,1)S(1)} collective-permute-done((f16[392,128]{1,0:T(8,128)(2,1)S(1)}, f16[392,128]{1,0:T(8,128)(2,1)S(1)}, u32[]{:S(2)}, u32[]{:S(2)}) %collective-permute-start) | collective-permute-done | bytes 100384 | tf_op jit(solution)/shard_map/ppermute | solution.py:199
  54.2 0.6 shard_map.19
  54.9 17.9 %all_to_all.11 = f16[16,32,256]{2,1,0:T(8,128)(2,1)S(1)} all-to-all(f16[16,32,256]{2,1,0:T(8,128)(2,1)S(1)} %convert_element_type.22), channel_id=1, replica_groups={{0,16,32,48,128,144,160,176,256,272,288,304,384,400,416,432},{64,80,96,..., dimensions={0} | all-to-all | bytes 524288 | tf_op jit(solution)/shard_map/all_to_all | solution.py:207
  72.8 0.1 convert.6.x_ref
  72.8 1.0 %shard_map.20 = f32[2,8,32,256]{3,2,1,0:T(8,128)} custom-call(f32[32,16,256]{2,1,0:T(8,128)S(1)} %convert.6.x_ref), custom_call_target="tpu_custom_call" | custom-call | tf_op jit(solution)/shard_map/pallas_call | solution.py:180
  (5 shorter events, 0.1 us)
Async XLA Ops:
  0.0 0.9 %copy-start = (bf16[2,8,128,64]{2,3,1,0:T(8,128)(2,1)S(1)}, bf16[2,8,128,64]{2,3,1,0:T(8,128)(2,1)}, u32[]{:S(2)}) copy-start(bf16[2,8,128,64]{2,3,1,0:T(8,128)(2,1)} %param.1) | copy-start | bytes 786436
  30.4 15.0 %collective-permute-start.1 = (f16[392,128]{1,0:T(8,128)(2,1)S(1)}, f16[392,128]{1,0:T(8,128)(2,1)S(1)}, u32[]{:S(2)}, u32[]{:S(2)}) collective-permute-start(f16[392,128]{1,0:T(8,128)(2,1)S(1)} %get-tuple-element.5), channel_id=1, source_target_pairs={{0,64},{1,65},{4,68},{5,69},{8,72},{9,73},{12,76},{13,77},{16,81},... | collective-permute-start | bytes 301064 | tf_op jit(solution)/shard_map/ppermute | solution.py:198
  39.0 15.3 %collective-permute-start = (f16[392,128]{1,0:T(8,128)(2,1)S(1)}, f16[392,128]{1,0:T(8,128)(2,1)S(1)}, u32[]{:S(2)}, u32[]{:S(2)}) collective-permute-start(f16[392,128]{1,0:T(8,128)(2,1)S(1)} %get-tuple-element.6), channel_id=1, source_target_pairs={{0,0},{1,1},{4,4},{5,5},{8,8},{9,9},{12,12},{13,13},{16,17},{17,16... | collective-permute-start | bytes 301064 | tf_op jit(solution)/shard_map/ppermute | solution.py:199

commit v4 on v3

--- a/solution.py
+++ b/solution.py
@@ -47,19 +47,24 @@
     return [[y * 8 + h * 4 + p for y in range(4) for p in range(4)] for h in range(2)]
 
 
-def exchange(x, dates):
-    rows = lax.broadcasted_iota(jnp.int32, x.shape, 0)
-    lanes = lax.broadcasted_iota(jnp.int32, x.shape, 1)
-    height, width = x.shape
-    step = dates // 2
-    while step:
-        low_row = (rows & step) == 0
-        low_lane = (lanes & (step * LOOK_COLS)) == 0
-        up = pltpu.roll(pltpu.roll(x, height - step, 0), step * LOOK_COLS, 1)
-        down = pltpu.roll(pltpu.roll(x, step, 0), width - step * LOOK_COLS, 1)
-        x = jnp.where(low_row == low_lane, x, jnp.where(low_row, up, down))
-        step //= 2
-    return x
+def exchange(x):
+    width = x.shape[2] // 2
+    low, high = x[:, :, :width], x[:, :, width:]
+    row = lax.broadcasted_iota(jnp.int32, low.shape, 1)
+    lane = lax.broadcasted_iota(jnp.int32, low.shape, 2) // LOOK_COLS
+    low, high = (
+        jnp.where(row < 4, low, pltpu.roll(high, 4, 1)),
+        jnp.where(row < 4, pltpu.roll(low, 4, 1), high),
+    )
+
+    def swap(x, bit):
+        step = bit * LOOK_COLS
+        up = pltpu.roll(pltpu.roll(x, LOOK_ROWS - bit, 1), step, 2)
+        down = pltpu.roll(pltpu.roll(x, bit, 1), width - step, 2)
+        low_row = (row & bit) == 0
+        return jnp.where(low_row == ((lane & bit) == 0), x, jnp.where(low_row, up, down))
+
+    return jnp.concatenate([swap(swap(low, 2), 1), swap(swap(high, 2), 1)], axis=2)
 
 
 def split_looks(x_ref, y_ref):
@@ -71,14 +76,13 @@
         for part in range(parts):
             block = x_ref[part, :, half * LOOK_COLS : (half + 1) * LOOK_COLS, :]
             block = block.reshape(dates * LOOK_COLS, rows).astype(jnp.float32)
-            block = exchange(block.T, dates)
-            blocks.append(block.reshape(look_rows, dates, dates * LOOK_COLS))
+            blocks.append(exchange(block.T.reshape(look_rows, LOOK_ROWS, dates * LOOK_COLS)))
         looks = jnp.concatenate(blocks, axis=1).astype(y_ref.dtype)
         for look_row in range(look_rows):
             y_ref[worked_at(look_row, half, tile)] = looks[look_row]
 
 
-def pairs(x_ref, y_ref):
+def pairs(x_ref, own_ref, other_ref):
     blocks, both, pixels = x_ref.shape
     dates = both // 2
     count = blocks * dates // 2
@@ -106,15 +110,23 @@
     bound = highest * lax.rsqrt(highest * highest + 1e-06)
     depth = jnp.clip(jnp.floor(-jnp.log2(bound + 1e-37)), 0.0, DEEPEST)
     factor = jnp.exp2(depth + SHIFT)
+    pieces = []
     for q in range(2):
-        place = q ^ h
         own = lax.rsqrt(power_i[q] * power_j[q] + 1e-06) * factor
         other = lax.rsqrt(power_i[q] * power_j[1 - q] + 1e-06) * factor
-        own_imag = cross(turned[q], one[q])
-        y_ref[place, :count] = jnp.where(i >= j, own_real[q], own_imag) * own
-        y_ref[place, count : 2 * count] = cross(one[q], one[1 - q]) * other
-        y_ref[place, 2 * count : 3 * count] = cross(turned[q], one[1 - q]) * other
-        y_ref[place, 3 * count :] = jnp.broadcast_to(depth, (EXTRA, count))
+        pieces.append(
+            (
+                jnp.where(i >= j, own_real[q], cross(turned[q], one[q])) * own,
+                cross(one[q], one[1 - q]) * other,
+                cross(turned[q], one[1 - q]) * other,
+            )
+        )
+    for block, (first, second) in enumerate(zip(*pieces)):
+        rows = slice(block * count, (block + 1) * count)
+        own_ref[rows] = jnp.where(h == 0, first, second)
+        other_ref[rows] = jnp.where(h == 0, second, first)
+    for y_ref in (own_ref, other_ref):
+        y_ref[3 * count :] = jnp.broadcast_to(depth, (EXTRA, count))
 
 
 def interleave(own, other, h):
@@ -176,12 +188,12 @@
     y_ref[1] = jnp.swapaxes(jnp.where(own, 0.0, imag * scale), 0, 1)
 
 
-def call(kernel, shape, dtype, *xs):
+def call(kernel, out_shape, *xs):
     return pl.pallas_call(
         kernel,
-        out_shape=jax.ShapeDtypeStruct(shape, dtype),
+        out_shape=out_shape,
         in_specs=[VMEM] * len(xs),
-        out_specs=VMEM,
+        out_specs=jax.tree.map(lambda _: VMEM, out_shape),
         compiler_params=pltpu.CompilerParams(vmem_limit_bytes=32 * 1024 * 1024),
     )(*xs)
 
@@ -192,21 +204,21 @@
     pixels = LOOK_ROWS * LOOK_COLS
     count = blocks * dates
     x = slc.transpose(0, 1, 3, 2)
-    x = call(split_looks, (blocks, parts * dates, pixels), jnp.bfloat16, x)
+    x = call(split_looks, jax.ShapeDtypeStruct((blocks, parts * dates, pixels), jnp.bfloat16), x)
     x = lax.all_to_all(x, "date", 0, 0, tiled=True)
-    x = call(pairs, (2, 3 * count // 2 + EXTRA, count // 2), jnp.float32, x)
-    other = lax.ppermute(x[1].astype(jnp.float16), ("date", "tile"), moves(False))
-    own = lax.ppermute(x[0].astype(jnp.float16), ("date", "tile"), moves(True))
+    shape = jax.ShapeDtypeStruct((3 * count // 2 + EXTRA, count // 2), jnp.float32)
+    own, other = call(pairs, (shape, shape), x)
+    other = lax.ppermute(other.astype(jnp.float16), ("date", "tile"), moves(False))
+    own = lax.ppermute(own.astype(jnp.float16), ("date", "tile"), moves(True))
     x = call(
         unfold,
-        (blocks // 2, 2 * parts * dates, count),
-        jnp.float32,
+        jax.ShapeDtypeStruct((blocks // 2, 2 * parts * dates, count), jnp.float32),
         own.astype(jnp.float32),
         other.astype(jnp.float32),
     )
     x = lax.all_to_all(x.astype(jnp.float16), "date", 0, 0, axis_index_groups=quads(), tiled=True)
     x = x.astype(jnp.float32).reshape(blocks, parts * dates, count)
-    return call(spread, (parts, dates, blocks, count), jnp.float32, x)
+    return call(spread, jax.ShapeDtypeStruct((parts, dates, blocks, count), jnp.float32), x)
 
 
 def solution(mesh):

time: 74.1 us -> 74 us (level)
  no operation moved by 1% of the time
where the time goes in v4:
time: 74 us; the launch traced here: 73.7 us
  blocking collectives  45.8 us (62%)
  starting transfers between devices  14.9 us (20%)
  waiting for transfers between devices  8.88 us (12%)
  Pallas kernels  2.95 us (4%)
  local copies, waits for them, and re-layouts  0.95 us (1%)
    all_to_all x1, blocking collectives, on_device(): x = lax.all_to_all(x, 'date', 0, 0, tiled=True)  27.9 us
    all_to_all x1, blocking collectives, on_device(): lax.all_to_all(x.astype(jnp.float16), 'date', 0, 0, axis_index_groups=qua...  17.9 us
    ppermute x1, waiting for transfers between devices, on_device(): own = lax.ppermute(own.astype(jnp.float16), ('date', 'tile'), moves(True))  8.86 us
    ppermute x1, starting transfers between devices, on_device(): lax.ppermute(other.astype(jnp.float16), ('date', 'tile'), moves(False))  8.6 us
    ppermute x1, starting transfers between devices, on_device(): own = lax.ppermute(own.astype(jnp.float16), ('date', 'tile'), moves(True))  6.34 us
    pallas_call x4, Pallas kernels, call(): pl.pallas_call(kernel, out_shape=out_shape, in_specs=[VMEM] * len(xs), ou...  2.95 us
  transfers between devices with their start and end apart: 2, of which 1 were waited for; matrix products, arithmetic and copies ran while one was open for 0% of the time, Pallas kernels for 0%

profile of v4, /device:TPU:128, one launch (start us, length us, event | category | flops | bytes accessed | tf_op | source)
XLA Modules:
  0.0 73.7 jit_solution(6196011784329638107)
XLA Ops:
  0.0 0.0 copy-start
  0.0 0.9 %copy-done = bf16[2,8,128,64]{2,3,1,0:T(8,128)(2,1)S(1)} copy-done((bf16[2,8,128,64]{2,3,1,0:T(8,128)(2,1)S(1)}, bf16[2,8,128,64]{2,3,1,0:T(8,128)(2,1)}, u32[]{:S(2)}) %copy-start) | copy-done | bytes 262168
  1.0 0.9 %shard_map.17 = bf16[32,16,256]{2,1,0:T(8,128)(2,1)S(1)} custom-call(bf16[2,8,64,128]{3,2,1,0:T(8,128)(2,1)S(1)} %bitcast.3), custom_call_target="tpu_custom_call" | custom-call | tf_op jit(solution)/shard_map/pallas_call | solution.py:192
  1.8 27.9 %all_to_all.10.x_ref = bf16[32,16,256]{2,1,0:T(8,128)(2,1)S(1)} all-to-all(bf16[32,16,256]{2,1,0:T(8,128)(2,1)S(1)} %shard_map.17), channel_id=1, replica_groups=mesh['date'=32,'tile'=16] {'date'}, dimensions={0} | all-to-all | bytes 524288 | tf_op jit(solution)/shard_map/all_to_all | solution.py:208
  29.7 0.4 shard_map.18
  30.2 8.6 %collective-permute-start.1 = (f16[392,128]{1,0:T(8,128)(2,1)S(1)}, f16[392,128]{1,0:T(8,128)(2,1)S(1)}, u32[]{:S(2)}, u32[]{:S(2)}) collective-permute-start(f16[392,128]{1,0:T(8,128)(2,1)S(1)} %convert_element_type.18), channel_id=1, source_target_pairs={{0,64},{1,65},{4,68},{5,69},{8,72},{9,73},{12,76},{13,77},{16,81},... | collective-permute-start | bytes 301064 | tf_op jit(solution)/shard_map/ppermute | solution.py:211
  38.8 6.3 %collective-permute-start = (f16[392,128]{1,0:T(8,128)(2,1)S(1)}, f16[392,128]{1,0:T(8,128)(2,1)S(1)}, u32[]{:S(2)}, u32[]{:S(2)}) collective-permute-start(f16[392,128]{1,0:T(8,128)(2,1)S(1)} %convert_element_type.16), channel_id=1, source_target_pairs={{0,0},{1,1},{4,4},{5,5},{8,8},{9,9},{12,12},{13,13},{16,17},{17,16... | collective-permute-start | bytes 301064 | tf_op jit(solution)/shard_map/ppermute | solution.py:212
  45.2 0.0 collective-permute-done.1
  45.2 8.9 %collective-permute-done = f16[392,128]{1,0:T(8,128)(2,1)S(1)} collective-permute-done((f16[392,128]{1,0:T(8,128)(2,1)S(1)}, f16[392,128]{1,0:T(8,128)(2,1)S(1)}, u32[]{:S(2)}, u32[]{:S(2)}) %collective-permute-start) | collective-permute-done | bytes 100384 | tf_op jit(solution)/shard_map/ppermute | solution.py:212
  54.1 0.6 shard_map.19
  54.7 17.9 %all_to_all.11 = f16[16,32,256]{2,1,0:T(8,128)(2,1)S(1)} all-to-all(f16[16,32,256]{2,1,0:T(8,128)(2,1)S(1)} %convert_element_type.20), channel_id=1, replica_groups={{0,16,32,48,128,144,160,176,256,272,288,304,384,400,416,432},{64,80,96,..., dimensions={0} | all-to-all | bytes 524288 | tf_op jit(solution)/shard_map/all_to_all | solution.py:219
  72.6 0.1 convert.1.x_ref
  72.7 1.0 %shard_map.20 = f32[2,8,32,256]{3,2,1,0:T(8,128)} custom-call(f32[32,16,256]{2,1,0:T(8,128)S(1)} %convert.1.x_ref), custom_call_target="tpu_custom_call" | custom-call | tf_op jit(solution)/shard_map/pallas_call | solution.py:192
  (5 shorter events, 0.1 us)
Async XLA Ops:
  0.0 0.9 %copy-start = (bf16[2,8,128,64]{2,3,1,0:T(8,128)(2,1)S(1)}, bf16[2,8,128,64]{2,3,1,0:T(8,128)(2,1)}, u32[]{:S(2)}) copy-start(bf16[2,8,128,64]{2,3,1,0:T(8,128)(2,1)} %param.1) | copy-start | bytes 786436
  30.2 15.0 %collective-permute-start.1 = (f16[392,128]{1,0:T(8,128)(2,1)S(1)}, f16[392,128]{1,0:T(8,128)(2,1)S(1)}, u32[]{:S(2)}, u32[]{:S(2)}) collective-permute-start(f16[392,128]{1,0:T(8,128)(2,1)S(1)} %convert_element_type.18), channel_id=1, source_target_pairs={{0,64},{1,65},{4,68},{5,69},{8,72},{9,73},{12,76},{13,77},{16,81},... | collective-permute-start | bytes 301064 | tf_op jit(solution)/shard_map/ppermute | solution.py:211
  38.8 15.2 %collective-permute-start = (f16[392,128]{1,0:T(8,128)(2,1)S(1)}, f16[392,128]{1,0:T(8,128)(2,1)S(1)}, u32[]{:S(2)}, u32[]{:S(2)}) collective-permute-start(f16[392,128]{1,0:T(8,128)(2,1)S(1)} %convert_element_type.16), channel_id=1, source_target_pairs={{0,0},{1,1},{4,4},{5,5},{8,8},{9,9},{12,12},{13,13},{16,17},{17,16... | collective-permute-start | bytes 301064 | tf_op jit(solution)/shard_map/ppermute | solution.py:212

commit v5 on v4

--- a/solution.py
+++ b/solution.py
@@ -26,7 +26,7 @@
     y = (tile // 4 - source // 4) % 4
     p = half * 2 + ((source % 2) ^ (tile % 2))
     cross = (source // 2 % 2) ^ (tile // 2 % 2)
-    return y * 4 + p, cross ^ h
+    return 15 - (y * 4 + p), cross ^ h
 
 
 def moves(own):
@@ -44,7 +44,7 @@
 
 
 def quads():
-    return [[y * 8 + h * 4 + p for y in range(4) for p in range(4)] for h in range(2)]
+    return [[y * 8 + h * 4 + p for y in range(3, -1, -1) for p in range(3, -1, -1)] for h in range(2)]
 
 
 def exchange(x):
@@ -163,8 +163,11 @@
         real = interleave(real, x_ref[count : 2 * count], h)
         imag = interleave(imag, x_ref[2 * count : 3 * count], h)
         first = piece * 2 * dates
-        y_ref[:, first : first + dates] = real.reshape(peers, dates, 2 * count)
-        y_ref[:, first + dates : first + 2 * dates] = imag.reshape(peers, dates, 2 * count)
+        real = real.reshape(peers, dates, 2 * count)
+        imag = imag.reshape(peers, dates, 2 * count)
+        for peer in range(peers):
+            y_ref[peers - 1 - peer, first : first + dates] = real[peer]
+            y_ref[peers - 1 - peer, first + dates : first + 2 * dates] = imag[peer]
 
 
 def spread(x_ref, y_ref):

time: 74 us -> 71.9 us (0.972)
  blocking collectives: 45.8 us -> 43.7 us
    all_to_all x1, blocking collectives: 17.9 us -> 15.8 us  [on_device(): lax.all_to_all(x.astype(jnp.float16), 'date', 0, 0, axis_index_groups=qua...]
where the time goes in v5:
time: 71.9 us; the launch traced here: 71.6 us
  blocking collectives  43.7 us (61%)
  starting transfers between devices  14.9 us (21%)
  waiting for transfers between devices  8.88 us (12%)
  Pallas kernels  2.96 us (4%)
  local copies, waits for them, and re-layouts  0.95 us (1%)
    all_to_all x1, blocking collectives, on_device(): x = lax.all_to_all(x, 'date', 0, 0, tiled=True)  27.9 us
    all_to_all x1, blocking collectives, on_device(): lax.all_to_all(x.astype(jnp.float16), 'date', 0, 0, axis_index_groups=qua...  15.8 us
    ppermute x1, waiting for transfers between devices, on_device(): own = lax.ppermute(own.astype(jnp.float16), ('date', 'tile'), moves(True))  8.86 us
    ppermute x1, starting transfers between devices, on_device(): lax.ppermute(other.astype(jnp.float16), ('date', 'tile'), moves(False))  8.6 us
    ppermute x1, starting transfers between devices, on_device(): own = lax.ppermute(own.astype(jnp.float16), ('date', 'tile'), moves(True))  6.34 us
    pallas_call x4, Pallas kernels, call(): pl.pallas_call(kernel, out_shape=out_shape, in_specs=[VMEM] * len(xs), ou...  2.96 us
  transfers between devices with their start and end apart: 2, of which 1 were waited for; matrix products, arithmetic and copies ran while one was open for 0% of the time, Pallas kernels for 0%

profile of v5, /device:TPU:128, one launch (start us, length us, event | category | flops | bytes accessed | tf_op | source)
XLA Modules:
  0.0 71.6 jit_solution(2276462360821813633)
XLA Ops:
  0.0 0.0 copy-start
  0.0 0.9 %copy-done = bf16[2,8,128,64]{2,3,1,0:T(8,128)(2,1)S(1)} copy-done((bf16[2,8,128,64]{2,3,1,0:T(8,128)(2,1)S(1)}, bf16[2,8,128,64]{2,3,1,0:T(8,128)(2,1)}, u32[]{:S(2)}) %copy-start) | copy-done | bytes 262168
  1.0 0.9 %shard_map.17 = bf16[32,16,256]{2,1,0:T(8,128)(2,1)S(1)} custom-call(bf16[2,8,64,128]{3,2,1,0:T(8,128)(2,1)S(1)} %bitcast.3), custom_call_target="tpu_custom_call" | custom-call | tf_op jit(solution)/shard_map/pallas_call | solution.py:195
  1.8 27.9 %all_to_all.10.x_ref = bf16[32,16,256]{2,1,0:T(8,128)(2,1)S(1)} all-to-all(bf16[32,16,256]{2,1,0:T(8,128)(2,1)S(1)} %shard_map.17), channel_id=1, replica_groups=mesh['date'=32,'tile'=16] {'date'}, dimensions={0} | all-to-all | bytes 524288 | tf_op jit(solution)/shard_map/all_to_all | solution.py:211
  29.7 0.4 shard_map.18
  30.2 8.6 %collective-permute-start.1 = (f16[392,128]{1,0:T(8,128)(2,1)S(1)}, f16[392,128]{1,0:T(8,128)(2,1)S(1)}, u32[]{:S(2)}, u32[]{:S(2)}) collective-permute-start(f16[392,128]{1,0:T(8,128)(2,1)S(1)} %convert_element_type.18), channel_id=1, source_target_pairs={{0,64},{1,65},{4,68},{5,69},{8,72},{9,73},{12,76},{13,77},{16,81},... | collective-permute-start | bytes 301064 | tf_op jit(solution)/shard_map/ppermute | solution.py:214
  38.8 6.3 %collective-permute-start = (f16[392,128]{1,0:T(8,128)(2,1)S(1)}, f16[392,128]{1,0:T(8,128)(2,1)S(1)}, u32[]{:S(2)}, u32[]{:S(2)}) collective-permute-start(f16[392,128]{1,0:T(8,128)(2,1)S(1)} %convert_element_type.16), channel_id=1, source_target_pairs={{0,0},{1,1},{4,4},{5,5},{8,8},{9,9},{12,12},{13,13},{16,17},{17,16... | collective-permute-start | bytes 301064 | tf_op jit(solution)/shard_map/ppermute | solution.py:215
  45.2 0.0 collective-permute-done.1
  45.2 8.9 %collective-permute-done = f16[392,128]{1,0:T(8,128)(2,1)S(1)} collective-permute-done((f16[392,128]{1,0:T(8,128)(2,1)S(1)}, f16[392,128]{1,0:T(8,128)(2,1)S(1)}, u32[]{:S(2)}, u32[]{:S(2)}) %collective-permute-start) | collective-permute-done | bytes 100384 | tf_op jit(solution)/shard_map/ppermute | solution.py:215
  54.1 0.6 shard_map.19
  54.7 15.8 %all_to_all.11 = f16[16,32,256]{2,1,0:T(8,128)(2,1)S(1)} all-to-all(f16[16,32,256]{2,1,0:T(8,128)(2,1)S(1)} %convert_element_type.20), channel_id=1, replica_groups={{432,416,400,384,304,288,272,256,176,160,144,128,48,32,16,0},{496,480,4..., dimensions={0} | all-to-all | bytes 524288 | tf_op jit(solution)/shard_map/all_to_all | solution.py:222
  70.5 0.1 convert.1.x_ref
  70.6 1.0 %shard_map.20 = f32[2,8,32,256]{3,2,1,0:T(8,128)} custom-call(f32[32,16,256]{2,1,0:T(8,128)S(1)} %convert.1.x_ref), custom_call_target="tpu_custom_call" | custom-call | tf_op jit(solution)/shard_map/pallas_call | solution.py:195
  (5 shorter events, 0.1 us)
Async XLA Ops:
  0.0 0.9 %copy-start = (bf16[2,8,128,64]{2,3,1,0:T(8,128)(2,1)S(1)}, bf16[2,8,128,64]{2,3,1,0:T(8,128)(2,1)}, u32[]{:S(2)}) copy-start(bf16[2,8,128,64]{2,3,1,0:T(8,128)(2,1)} %param.1) | copy-start | bytes 786436
  30.2 15.0 %collective-permute-start.1 = (f16[392,128]{1,0:T(8,128)(2,1)S(1)}, f16[392,128]{1,0:T(8,128)(2,1)S(1)}, u32[]{:S(2)}, u32[]{:S(2)}) collective-permute-start(f16[392,128]{1,0:T(8,128)(2,1)S(1)} %convert_element_type.18), channel_id=1, source_target_pairs={{0,64},{1,65},{4,68},{5,69},{8,72},{9,73},{12,76},{13,77},{16,81},... | collective-permute-start | bytes 301064 | tf_op jit(solution)/shard_map/ppermute | solution.py:214
  38.8 15.2 %collective-permute-start = (f16[392,128]{1,0:T(8,128)(2,1)S(1)}, f16[392,128]{1,0:T(8,128)(2,1)S(1)}, u32[]{:S(2)}, u32[]{:S(2)}) collective-permute-start(f16[392,128]{1,0:T(8,128)(2,1)S(1)} %convert_element_type.16), channel_id=1, source_target_pairs={{0,0},{1,1},{4,4},{5,5},{8,8},{9,9},{12,12},{13,13},{16,17},{17,16... | collective-permute-start | bytes 301064 | tf_op jit(solution)/shard_map/ppermute | solution.py:215

commit v6 on v5

--- a/solution.py
+++ b/solution.py
@@ -15,10 +15,18 @@
 VMEM = pl.BlockSpec(memory_space=pltpu.VMEM)
 
 
+def order(y, z_lo):
+    return 31 - (jnp.where(z_lo < 4, 2 * z_lo, 15 - 2 * z_lo) * 4 + y)
+
+
+def middle_first():
+    return [y * 8 + z_lo for z_lo in (4, 3, 5, 2, 6, 1, 7, 0) for y in (3, 2, 1, 0)]
+
+
 def worked_at(look_row, half, tile):
     y = (look_row // 4 - tile // 4) % 4
     cross = (look_row // 2 % 2) ^ (tile // 2 % 2)
-    return y * 8 + cross * 4 + half * 2 + ((look_row % 2) ^ (tile % 2))
+    return order(y, cross * 4 + half * 2 + ((look_row % 2) ^ (tile % 2)))
 
 
 def found_at(look_col, tile, h):
@@ -26,7 +34,8 @@
     y = (tile // 4 - source // 4) % 4
     p = half * 2 + ((source % 2) ^ (tile % 2))
     cross = (source // 2 % 2) ^ (tile // 2 % 2)
-    return 15 - (y * 4 + p), cross ^ h
+    turn = jnp.where(p == 2, 0, jnp.where(p == 1, 1, jnp.where(p == 3, 2, 3)))
+    return (3 - y) * 4 + turn, cross ^ h
 
 
 def moves(own):
@@ -43,8 +52,11 @@
     return pairs
 
 
+SEATS = [y * 4 + p for y in (3, 2, 1, 0) for p in (2, 1, 3, 0)]
+
+
 def quads():
-    return [[y * 8 + h * 4 + p for y in range(3, -1, -1) for p in range(3, -1, -1)] for h in range(2)]
+    return [[seat // 4 * 8 + h * 4 + seat % 4 for seat in SEATS] for h in range(2)]
 
 
 def exchange(x):
@@ -87,7 +99,8 @@
     dates = both // 2
     count = blocks * dates // 2
     h = lax.axis_index("date") % 8 // 4
-    x = x_ref[...].astype(jnp.float32).reshape(4, 2, 4, both, pixels)
+    places = [middle_first().index(date) for date in range(blocks)]
+    x = jnp.stack([x_ref[place] for place in places]).astype(jnp.float32).reshape(4, 2, 4, both, pixels)
     one, turned, power_i, power_j = [], [], [], []
     dims = (((1,), (1,)), ((), ()))
 
@@ -165,9 +178,9 @@
         first = piece * 2 * dates
         real = real.reshape(peers, dates, 2 * count)
         imag = imag.reshape(peers, dates, 2 * count)
-        for peer in range(peers):
-            y_ref[peers - 1 - peer, first : first + dates] = real[peer]
-            y_ref[peers - 1 - peer, first + dates : first + 2 * dates] = imag[peer]
+        for place, peer in enumerate(SEATS):
+            y_ref[place, first : first + dates] = real[peer]
+            y_ref[place, first + dates : first + 2 * dates] = imag[peer]
 
 
 def spread(x_ref, y_ref):
@@ -208,7 +221,7 @@
     count = blocks * dates
     x = slc.transpose(0, 1, 3, 2)
     x = call(split_looks, jax.ShapeDtypeStruct((blocks, parts * dates, pixels), jnp.bfloat16), x)
-    x = lax.all_to_all(x, "date", 0, 0, tiled=True)
+    x = lax.all_to_all(x, "date", 0, 0, axis_index_groups=[middle_first()], tiled=True)
     shape = jax.ShapeDtypeStruct((3 * count // 2 + EXTRA, count // 2), jnp.float32)
     own, other = call(pairs, (shape, shape), x)
     other = lax.ppermute(other.astype(jnp.float16), ("date", "tile"), moves(False))

time: 71.9 us -> 67.9 us (0.944)
  the two profiles are of different devices: /device:TPU:128 before, /device:TPU:132 now
where the time goes in v6:
time: 67.9 us; the launch traced here: 67.7 us
  blocking collectives  39.2 us (58%)
  starting transfers between devices  12.4 us (18%)
  waiting for transfers between devices  11.9 us (18%)
  Pallas kernels  2.98 us (4%)
  local copies, waits for them, and re-layouts  0.95 us (1%)
    all_to_all x1, blocking collectives, on_device(): lax.all_to_all(x, 'date', 0, 0, axis_index_groups=[middle_first()], tiled...  24.1 us
    all_to_all x1, blocking collectives, on_device(): lax.all_to_all(x.astype(jnp.float16), 'date', 0, 0, axis_index_groups=qua...  15.1 us
    ppermute x1, waiting for transfers between devices, on_device(): own = lax.ppermute(own.astype(jnp.float16), ('date', 'tile'), moves(True))  11.9 us
    ppermute x1, starting transfers between devices, on_device(): lax.ppermute(other.astype(jnp.float16), ('date', 'tile'), moves(False))  7.73 us
    ppermute x1, starting transfers between devices, on_device(): own = lax.ppermute(own.astype(jnp.float16), ('date', 'tile'), moves(True))  4.71 us
    pallas_call x4, Pallas kernels, call(): pl.pallas_call(kernel, out_shape=out_shape, in_specs=[VMEM] * len(xs), ou...  2.98 us
  transfers between devices with their start and end apart: 2, of which 1 were waited for; matrix products, arithmetic and copies ran while one was open for 0% of the time, Pallas kernels for 0%

profile of v6, /device:TPU:132, one launch (start us, length us, event | category | flops | bytes accessed | tf_op | source)
XLA Modules:
  0.0 67.7 jit_solution(6141571533180864417)
XLA Ops:
  0.0 0.0 copy-start
  0.0 0.9 %copy-done = bf16[2,8,128,64]{2,3,1,0:T(8,128)(2,1)S(1)} copy-done((bf16[2,8,128,64]{2,3,1,0:T(8,128)(2,1)S(1)}, bf16[2,8,128,64]{2,3,1,0:T(8,128)(2,1)}, u32[]{:S(2)}) %copy-start) | copy-done | bytes 262168
  1.0 0.9 %shard_map.17 = bf16[32,16,256]{2,1,0:T(8,128)(2,1)S(1)} custom-call(bf16[2,8,64,128]{3,2,1,0:T(8,128)(2,1)S(1)} %bitcast.3), custom_call_target="tpu_custom_call" | custom-call | tf_op jit(solution)/shard_map/pallas_call | solution.py:208
  1.8 24.1 %all_to_all.10.x_ref = bf16[32,16,256]{2,1,0:T(8,128)(2,1)S(1)} all-to-all(bf16[32,16,256]{2,1,0:T(8,128)(2,1)S(1)} %shard_map.17), channel_id=1, replica_groups={{448,320,192,64,432,304,176,48,464,336,208,80,416,288,160,32,480,352,22..., dimensions={0} | all-to-all | bytes 524288 | tf_op jit(solution)/shard_map/all_to_all | solution.py:224
  25.9 0.4 shard_map.18
  26.4 7.7 %collective-permute-start.1 = (f16[392,128]{1,0:T(8,128)(2,1)S(1)}, f16[392,128]{1,0:T(8,128)(2,1)S(1)}, u32[]{:S(2)}, u32[]{:S(2)}) collective-permute-start(f16[392,128]{1,0:T(8,128)(2,1)S(1)} %convert_element_type.18), channel_id=1, source_target_pairs={{0,64},{1,65},{4,68},{5,69},{8,72},{9,73},{12,76},{13,77},{16,81},... | collective-permute-start | bytes 301064 | tf_op jit(solution)/shard_map/ppermute | solution.py:227
  34.2 4.7 %collective-permute-start = (f16[392,128]{1,0:T(8,128)(2,1)S(1)}, f16[392,128]{1,0:T(8,128)(2,1)S(1)}, u32[]{:S(2)}, u32[]{:S(2)}) collective-permute-start(f16[392,128]{1,0:T(8,128)(2,1)S(1)} %convert_element_type.16), channel_id=1, source_target_pairs={{0,0},{1,1},{4,4},{5,5},{8,8},{9,9},{12,12},{13,13},{16,17},{17,16... | collective-permute-start | bytes 301064 | tf_op jit(solution)/shard_map/ppermute | solution.py:228
  38.9 0.0 collective-permute-done.1
  38.9 11.9 %collective-permute-done = f16[392,128]{1,0:T(8,128)(2,1)S(1)} collective-permute-done((f16[392,128]{1,0:T(8,128)(2,1)S(1)}, f16[392,128]{1,0:T(8,128)(2,1)S(1)}, u32[]{:S(2)}, u32[]{:S(2)}) %collective-permute-start) | collective-permute-done | bytes 100384 | tf_op jit(solution)/shard_map/ppermute | solution.py:228
  50.8 0.6 shard_map.19
  51.5 15.1 %all_to_all.11 = f16[16,32,256]{2,1,0:T(8,128)(2,1)S(1)} all-to-all(f16[16,32,256]{2,1,0:T(8,128)(2,1)S(1)} %convert_element_type.20), channel_id=1, replica_groups={{416,400,432,384,288,272,304,256,160,144,176,128,32,16,48,0},{480,464,4..., dimensions={0} | all-to-all | bytes 524288 | tf_op jit(solution)/shard_map/all_to_all | solution.py:235
  66.6 0.1 convert.1.x_ref
  66.7 1.1 %shard_map.20 = f32[2,8,32,256]{3,2,1,0:T(8,128)} custom-call(f32[32,16,256]{2,1,0:T(8,128)S(1)} %convert.1.x_ref), custom_call_target="tpu_custom_call" | custom-call | tf_op jit(solution)/shard_map/pallas_call | solution.py:208
  (5 shorter events, 0.1 us)
Async XLA Ops:
  0.0 0.9 %copy-start = (bf16[2,8,128,64]{2,3,1,0:T(8,128)(2,1)S(1)}, bf16[2,8,128,64]{2,3,1,0:T(8,128)(2,1)}, u32[]{:S(2)}) copy-start(bf16[2,8,128,64]{2,3,1,0:T(8,128)(2,1)} %param.1) | copy-start | bytes 786436
  26.4 12.5 %collective-permute-start.1 = (f16[392,128]{1,0:T(8,128)(2,1)S(1)}, f16[392,128]{1,0:T(8,128)(2,1)S(1)}, u32[]{:S(2)}, u32[]{:S(2)}) collective-permute-start(f16[392,128]{1,0:T(8,128)(2,1)S(1)} %convert_element_type.18), channel_id=1, source_target_pairs={{0,64},{1,65},{4,68},{5,69},{8,72},{9,73},{12,76},{13,77},{16,81},... | collective-permute-start | bytes 301064 | tf_op jit(solution)/shard_map/ppermute | solution.py:227
  34.2 16.6 %collective-permute-start = (f16[392,128]{1,0:T(8,128)(2,1)S(1)}, f16[392,128]{1,0:T(8,128)(2,1)S(1)}, u32[]{:S(2)}, u32[]{:S(2)}) collective-permute-start(f16[392,128]{1,0:T(8,128)(2,1)S(1)} %convert_element_type.16), channel_id=1, source_target_pairs={{0,0},{1,1},{4,4},{5,5},{8,8},{9,9},{12,12},{13,13},{16,17},{17,16... | collective-permute-start | bytes 301064 | tf_op jit(solution)/shard_map/ppermute | solution.py:228

commit v7 on v6

--- a/solution.py
+++ b/solution.py
@@ -35,7 +35,7 @@
     p = half * 2 + ((source % 2) ^ (tile % 2))
     cross = (source // 2 % 2) ^ (tile // 2 % 2)
     turn = jnp.where(p == 2, 0, jnp.where(p == 1, 1, jnp.where(p == 3, 2, 3)))
-    return (3 - y) * 4 + turn, cross ^ h
+    return turn * 4 + 3 - y, cross ^ h
 
 
 def moves(own):
@@ -52,7 +52,7 @@
     return pairs
 
 
-SEATS = [y * 4 + p for y in (3, 2, 1, 0) for p in (2, 1, 3, 0)]
+SEATS = [y * 4 + p for p in (2, 1, 3, 0) for y in (3, 2, 1, 0)]
 
 
 def quads():

time: 67.9 us -> 68 us (level)
  the two profiles are of different devices: /device:TPU:132 before, /device:TPU:130 now
where the time goes in v7:
time: 68 us; the launch traced here: 67.8 us
  blocking collectives  39.3 us (58%)
  starting transfers between devices  12.4 us (18%)
  waiting for transfers between devices  11.9 us (18%)
  Pallas kernels  2.98 us (4%)
  local copies, waits for them, and re-layouts  0.95 us (1%)
    all_to_all x1, blocking collectives, on_device(): lax.all_to_all(x, 'date', 0, 0, axis_index_groups=[middle_first()], tiled...  24.1 us
    all_to_all x1, blocking collectives, on_device(): lax.all_to_all(x.astype(jnp.float16), 'date', 0, 0, axis_index_groups=qua...  15.2 us
    ppermute x1, waiting for transfers between devices, on_device(): own = lax.ppermute(own.astype(jnp.float16), ('date', 'tile'), moves(True))  11.9 us
    ppermute x1, starting transfers between devices, on_device(): lax.ppermute(other.astype(jnp.float16), ('date', 'tile'), moves(False))  7.73 us
    ppermute x1, starting transfers between devices, on_device(): own = lax.ppermute(own.astype(jnp.float16), ('date', 'tile'), moves(True))  4.71 us
    pallas_call x4, Pallas kernels, call(): pl.pallas_call(kernel, out_shape=out_shape, in_specs=[VMEM] * len(xs), ou...  2.98 us
  transfers between devices with their start and end apart: 2, of which 1 were waited for; matrix products, arithmetic and copies ran while one was open for 0% of the time, Pallas kernels for 0%

profile of v7, /device:TPU:130, one launch (start us, length us, event | category | flops | bytes accessed | tf_op | source)
XLA Modules:
  0.0 67.8 jit_solution(257616391317242801)
XLA Ops:
  0.0 0.0 copy-start
  0.0 0.9 %copy-done = bf16[2,8,128,64]{2,3,1,0:T(8,128)(2,1)S(1)} copy-done((bf16[2,8,128,64]{2,3,1,0:T(8,128)(2,1)S(1)}, bf16[2,8,128,64]{2,3,1,0:T(8,128)(2,1)}, u32[]{:S(2)}) %copy-start) | copy-done | bytes 262168
  1.0 0.9 %shard_map.17 = bf16[32,16,256]{2,1,0:T(8,128)(2,1)S(1)} custom-call(bf16[2,8,64,128]{3,2,1,0:T(8,128)(2,1)S(1)} %bitcast.3), custom_call_target="tpu_custom_call" | custom-call | tf_op jit(solution)/shard_map/pallas_call | solution.py:208
  1.8 24.1 %all_to_all.10.x_ref = bf16[32,16,256]{2,1,0:T(8,128)(2,1)S(1)} all-to-all(bf16[32,16,256]{2,1,0:T(8,128)(2,1)S(1)} %shard_map.17), channel_id=1, replica_groups={{448,320,192,64,432,304,176,48,464,336,208,80,416,288,160,32,480,352,22..., dimensions={0} | all-to-all | bytes 524288 | tf_op jit(solution)/shard_map/all_to_all | solution.py:224
  25.9 0.4 shard_map.18
  26.4 7.7 %collective-permute-start.1 = (f16[392,128]{1,0:T(8,128)(2,1)S(1)}, f16[392,128]{1,0:T(8,128)(2,1)S(1)}, u32[]{:S(2)}, u32[]{:S(2)}) collective-permute-start(f16[392,128]{1,0:T(8,128)(2,1)S(1)} %convert_element_type.18), channel_id=1, source_target_pairs={{0,64},{1,65},{4,68},{5,69},{8,72},{9,73},{12,76},{13,77},{16,81},... | collective-permute-start | bytes 301064 | tf_op jit(solution)/shard_map/ppermute | solution.py:227
  34.2 4.7 %collective-permute-start = (f16[392,128]{1,0:T(8,128)(2,1)S(1)}, f16[392,128]{1,0:T(8,128)(2,1)S(1)}, u32[]{:S(2)}, u32[]{:S(2)}) collective-permute-start(f16[392,128]{1,0:T(8,128)(2,1)S(1)} %convert_element_type.16), channel_id=1, source_target_pairs={{0,0},{1,1},{4,4},{5,5},{8,8},{9,9},{12,12},{13,13},{16,17},{17,16... | collective-permute-start | bytes 301064 | tf_op jit(solution)/shard_map/ppermute | solution.py:228
  38.9 0.0 collective-permute-done.1
  38.9 11.9 %collective-permute-done = f16[392,128]{1,0:T(8,128)(2,1)S(1)} collective-permute-done((f16[392,128]{1,0:T(8,128)(2,1)S(1)}, f16[392,128]{1,0:T(8,128)(2,1)S(1)}, u32[]{:S(2)}, u32[]{:S(2)}) %collective-permute-start) | collective-permute-done | bytes 100384 | tf_op jit(solution)/shard_map/ppermute | solution.py:228
  50.8 0.6 shard_map.19
  51.5 15.2 %all_to_all.11 = f16[16,32,256]{2,1,0:T(8,128)(2,1)S(1)} all-to-all(f16[16,32,256]{2,1,0:T(8,128)(2,1)S(1)} %convert_element_type.20), channel_id=1, replica_groups={{416,288,160,32,400,272,144,16,432,304,176,48,384,256,128,0},{480,352,2..., dimensions={0} | all-to-all | bytes 524288 | tf_op jit(solution)/shard_map/all_to_all | solution.py:235
  66.7 0.1 convert.1.x_ref
  66.7 1.1 %shard_map.20 = f32[2,8,32,256]{3,2,1,0:T(8,128)} custom-call(f32[32,16,256]{2,1,0:T(8,128)S(1)} %convert.1.x_ref), custom_call_target="tpu_custom_call" | custom-call | tf_op jit(solution)/shard_map/pallas_call | solution.py:208
  (5 shorter events, 0.1 us)
Async XLA Ops:
  0.0 0.9 %copy-start = (bf16[2,8,128,64]{2,3,1,0:T(8,128)(2,1)S(1)}, bf16[2,8,128,64]{2,3,1,0:T(8,128)(2,1)}, u32[]{:S(2)}) copy-start(bf16[2,8,128,64]{2,3,1,0:T(8,128)(2,1)} %param.1) | copy-start | bytes 786436
  26.4 12.5 %collective-permute-start.1 = (f16[392,128]{1,0:T(8,128)(2,1)S(1)}, f16[392,128]{1,0:T(8,128)(2,1)S(1)}, u32[]{:S(2)}, u32[]{:S(2)}) collective-permute-start(f16[392,128]{1,0:T(8,128)(2,1)S(1)} %convert_element_type.18), channel_id=1, source_target_pairs={{0,64},{1,65},{4,68},{5,69},{8,72},{9,73},{12,76},{13,77},{16,81},... | collective-permute-start | bytes 301064 | tf_op jit(solution)/shard_map/ppermute | solution.py:227
  34.2 16.6 %collective-permute-start = (f16[392,128]{1,0:T(8,128)(2,1)S(1)}, f16[392,128]{1,0:T(8,128)(2,1)S(1)}, u32[]{:S(2)}, u32[]{:S(2)}) collective-permute-start(f16[392,128]{1,0:T(8,128)(2,1)S(1)} %convert_element_type.16), channel_id=1, source_target_pairs={{0,0},{1,1},{4,4},{5,5},{8,8},{9,9},{12,12},{13,13},{16,17},{17,16... | collective-permute-start | bytes 301064 | tf_op jit(solution)/shard_map/ppermute | solution.py:228
